TPU v7x, 512 devices: a whole 4x8x8 slice. The times are simulated.
512 devices in a mesh: dp: 32 (over z, x_hi, core), tensor: 16 (over x_lo, y).
Axes of the slice: x: 4 (x_hi: 2, x_lo: 2; x = x_hi * 2 + x_lo), y: 8, z: 8, core: 2. Of those that a mesh axis runs over, the one named last changes fastest.
Arguments:
- gate_pre: bfloat16 [4096, 14336], P('dp', 'tensor'), may hold values from -6 to 6
- up_pre: bfloat16 [4096, 14336], P('dp', 'tensor'), may hold values from -6 to 6
- cotangent: bfloat16 [4096, 4096], P('dp', 'tensor'), may hold values from -6 to 6
- weight_tiles: bfloat16 [16, 96, 128, 128], P('tensor', 'dp'), may hold values from -0.109375 to 0.109375
- tile_slots: int32 [16, 96], P('tensor', 'dp'), may hold values from 0 to 223, as said below
- live_counts: int32 [16], P('tensor'), may hold values from 24 to 96, as said below
Outputs:
- projected: bfloat16 [4096, 4096], P('dp', 'tensor')
- gate_grad: bfloat16 [4096, 14336], P('dp', 'tensor')
- up_grad: bfloat16 [4096, 14336], P('dp', 'tensor')
- tile_grad: float32 [16, 96, 128, 128], P('tensor', 'dp')
Inputs may be any that keep to these rules, and one draw needn't show every extreme that they name: `tile_slots`: within one tensor shard all 96 entries are distinct. `live_counts`: some shard has all 96 slots live.
All inputs are finite; a program needn't handle non-finite values.
Results may differ from a plain program's by a relative error of at most 0.019.
Values may be sent and summed in bfloat16 or wider, within the bound.
A program may use at most 64 MiB of HBM per device.

v0:
```python
import jax
import jax.numpy as jnp
from jax import lax
from jax.sharding import PartitionSpec as P


def per_device(gate_pre, up_pre, cotangent, weight_tiles, tile_slots, live_counts):
    tok_rows = gate_pre.shape[0]
    hid_width = gate_pre.shape[1]
    tile_edge = weight_tiles.shape[2]
    hid_blocks = hid_width // tile_edge
    shards = lax.axis_size("tensor")
    local_blocks = cotangent.shape[1] // tile_edge
    model_blocks = local_blocks * shards
    token_scale = (tok_rows * lax.axis_size("dp")) ** (-0.5)
    group_size = 16
    gate_val = gate_pre.astype(jnp.float32)
    up_val = up_pre.astype(jnp.float32)
    gate_sig = jax.nn.sigmoid(gate_val)
    silu_val = gate_val * gate_sig
    hidden = (silu_val * up_val).astype(jnp.bfloat16)
    hidden_blocks = hidden.reshape(tok_rows, hid_blocks, tile_edge).transpose(1, 0, 2)
    fetched_tiles, fetched_slots = (
        lax.all_gather(weight_tiles, "dp", axis=1, tiled=True),
        lax.all_gather(tile_slots, "dp", axis=1, tiled=True),
    )
    all_tiles = fetched_tiles[0]
    all_slots = fetched_slots[0]
    capacity = all_tiles.shape[0]
    live_count = live_counts[0]
    groups = capacity // group_size

    def forward_group(group_index, totals):
        offset = group_index * group_size
        group_tiles = lax.dynamic_slice_in_dim(all_tiles, offset, group_size, 0)
        group_slots = lax.dynamic_slice_in_dim(all_slots, offset, group_size, 0)
        is_live = offset + jnp.arange(group_size, dtype=jnp.int32) < live_count
        hid_index = group_slots // model_blocks
        mod_index = group_slots % model_blocks
        picked = hidden_blocks[hid_index]
        product = jnp.einsum(
            "gtb,gbc->gtc", picked, group_tiles, preferred_element_type=jnp.float32
        )
        product = jnp.where(is_live[:, None, None], product, 0.0)
        return totals.at[mod_index].add(product)

    sums = lax.fori_loop(
        0, groups, forward_group, jnp.zeros((model_blocks, tok_rows, tile_edge), jnp.float32)
    )
    shared = sums.astype(jnp.bfloat16).reshape(1, model_blocks, tok_rows, tile_edge)
    received = lax.all_to_all(shared, "tensor", split_axis=1, concat_axis=0, tiled=True)
    column_total = jnp.sum(received.astype(jnp.float32), axis=0)
    projected = (
        column_total.transpose(1, 0, 2)
        .reshape(tok_rows, local_blocks * tile_edge)
        .astype(jnp.bfloat16)
    )
    cot_local = cotangent.reshape(tok_rows, local_blocks, tile_edge).transpose(1, 0, 2)
    all_cot = lax.all_gather(cot_local, "tensor", axis=0, tiled=True)
    part_tiles = lax.all_gather(weight_tiles, "dp", axis=1, tiled=True)[0]
    part_slots = lax.all_gather(tile_slots, "dp", axis=1, tiled=True)[0]
    hidden_grad = jnp.zeros((hid_blocks, tok_rows, tile_edge), jnp.float32)
    grad_buffer = jnp.zeros((capacity, tile_edge, tile_edge), jnp.float32)
    count_here = part_tiles.shape[0]
    is_live = jnp.arange(count_here, dtype=jnp.int32) < live_count
    hid_index = part_slots // model_blocks
    mod_index = part_slots % model_blocks
    picked = hidden_blocks[hid_index]
    cot_picked = all_cot[mod_index]
    back = jnp.einsum("gtc,gbc->gtb", cot_picked, part_tiles, preferred_element_type=jnp.float32)
    back = jnp.where(is_live[:, None, None], back, 0.0)
    hidden_grad = hidden_grad.at[hid_index].add(back)
    tile_terms = (
        jnp.einsum("gtb,gtc->gbc", picked, cot_picked, preferred_element_type=jnp.float32)
        * token_scale
    )
    tile_terms = jnp.where(is_live[:, None, None], tile_terms, 0.0)
    grad_buffer = lax.dynamic_update_slice_in_dim(grad_buffer, tile_terms, jnp.int32(0), 0)
    hidden_grad, grad_buffer = (hidden_grad, grad_buffer)
    tile_grad = lax.psum_scatter(
        grad_buffer.reshape(1, capacity, tile_edge, tile_edge).astype(jnp.bfloat16),
        "dp",
        scatter_dimension=1,
        tiled=True,
    ).astype(jnp.float32)
    flat_grad = hidden_grad.transpose(1, 0, 2).reshape(tok_rows, hid_width)
    gate_grad = (flat_grad * up_val * gate_sig * (1.0 + gate_val * (1.0 - gate_sig))).astype(
        jnp.bfloat16
    )
    up_grad = (flat_grad * silu_val).astype(jnp.bfloat16)
    return (projected, gate_grad, up_grad, tile_grad)


def solution(mesh):
    in_specs = (
        P("dp", "tensor"),
        P("dp", "tensor"),
        P("dp", "tensor"),
        P("tensor", "dp", None, None),
        P("tensor", "dp"),
        P("tensor"),
    )
    out_specs = (
        P("dp", "tensor"),
        P("dp", "tensor"),
        P("dp", "tensor"),
        P("tensor", "dp", None, None),
    )
    return jax.shard_map(
        per_device, mesh=mesh, in_specs=in_specs, out_specs=out_specs, check_vma=False
    )
```

profile of v0, /device:TPU:1, one launch (start us, length us, event | category | flops | bytes accessed | tf_op | source)
XLA Modules:
  0.0 344.7 jit_solution(15729898504732721188)
XLA Ops:
  7.2 0.0 all-gather.5.cloned.1.call-start
  7.2 0.9 copy.40
  8.2 0.7 copy.41
  8.9 0.0 all-gather.5.cloned.1.call-update
  8.9 0.0 all-gather.3.cloned.1.call-start
  9.0 0.7 all-gather.3.cloned.1.call-update
  9.7 0.0 reduce-scatter.2.cloned.1.call-start
  10.4 1.1 copy.35
  11.5 1.8 copy.36
  13.3 1.3 dynamic-slice
  15.2 0.8 bitcast_dynamic-update-slice_fusion
  15.9 21.7 %all-reduce = s32[96]{0:T(128)S(1)} all-reduce(s32[96]{0:T(128)S(1)} %bitcast_dynamic-update-slice_fusion), channel_id=1, replica_groups=mesh['dp'=32,'tensor'=16] {'dp'}, use_global_device_ids=true, to_apply=%add | all-reduce | flops 96 | bytes 768 | tf_op jit(solution)/shard_map/squeeze | solution.py:28
  37.7 40.0 %all-gather.5.cloned.1.call-done = bf16[32,128,128]{2,1,0:T(8,128)(2,1)} async-done(((bf16[2,128,128]{2,1,0:T(8,128)(2,1)}), bf16[32,128,128]{2,1,0:T(8,128)(2,1)}) %all-gather.5.cloned.1.call-update) | async-done | bytes 1048592 | tf_op jit(solution)/shard_map/all_gather | solution.py:59
  77.7 2.4 gather_fusion.1
  80.1 98.9 %all-gather.3.cloned.1.call-done = bf16[1,96,128,128]{3,2,0,1:T(8,128)(2,1)} async-done(((bf16[1,3,128,128]{3,2,0,1:T(8,128)(2,1)}), bf16[1,96,128,128]{3,2,0,1:T(8,128)(2,1)}) %all-gather.3.cloned.1.call-update) | async-done | bytes 3145744 | tf_op jit(solution)/shard_map/all_gather | solution.py:24
  179.0 6.8 %broadcast_select_fusion = f32[96,128,128]{2,1,0:T(8,128)} fusion(pred[96]{0:T(512)(128)(4,1)S(1)} %iota_compare_fusion, bf16[96,128,128]{2,1,0:T(8,128)(2,1)S(1)} %gather_fusion.1, bf16[1,96,128,128]{3,2,0,1:T(8,128)(2,1)} %all-gather.3.cloned.1.call-done), kind=kOutput, calls=%fused_computation.19 | convolution fusion | flops 404226048 | bytes 12583008 | tf_op jit(solution)/shard_map/gtc,gbc->gtb/dot_general | solution.py:70
  185.8 12.9 %scatter_fusion.1 = f32[7,128,128]{2,1,0:T(8,128)S(1)} fusion(f32[7,128,128]{2,1,0:T(8,128)S(1)} %broadcast_in_dim.84, s32[96]{0:T(128)S(1)} %get-tuple-element.220, f32[96,128,128]{2,1,0:T(8,128)} %broadcast_select_fusion), kind=kCustom, calls=%fused_computation.4 | custom fusion | flops 1572864 | bytes 18874752 | tf_op jit(solution)/shard_map/scatter-add | solution.py:72
  198.7 0.2 copy.42
  198.9 0.3 fusion.11
  199.2 0.2 copy.38
  199.4 2.7 gather_fusion.2
  202.1 5.5 %fusion.2 = bf16[1,96,128,128]{3,2,1,0:T(8,128)(2,1)} fusion(pred[96]{0:T(512)(128)(4,1)S(1)} %iota_compare_fusion, bf16[96,128,128]{1,2,0:T(8,128)(2,1)} %gather_fusion.2, bf16[96,128,128]{2,1,0:T(8,128)(2,1)} %copy-done), kind=kOutput, calls=%fused_computation.18 | convolution fusion | flops 407371776 | bytes 9437280 | tf_op jit(solution)/shard_map/gtb,gtc->gbc/dot_general | solution.py:74
  207.7 1.6 broadcast_in_dim.83
  209.3 37.1 %while.15 = (s32[]{:T(128)}, f32[32,128,128]{2,1,0:T(8,128)}, s32[96]{0:T(128)S(1)}, s32[]{:T(128)}, bf16[7,128,128]{2,1,0:T(8,128)(2,1)S(1)}, /*index=5*/bf16[9...) while((s32[]{:T(128)}, f32[32,128,128]{2,1,0:T(8,128)}, s32[96]{0:T(128)S(1)}, ...), condition=%wide.region_2.3_spmd, body=%wide.region_0.2_spmd.sunk | while | flops 67634632 | bytes 6296259 | solution.py:47
  209.3 0.1 compare_select_fusion.13
  209.3 0.6 gather_fusion
  210.0 0.7 add_compare_fusion.2
  210.7 1.3 convolution_select_fusion.2
  212.0 3.4 scatter_fusion
  215.4 0.1 compare_select_fusion.13
  215.5 0.6 gather_fusion
  216.2 0.7 add_compare_fusion.2
  216.8 1.3 convolution_select_fusion.2
  218.2 3.4 scatter_fusion
  221.6 0.1 compare_select_fusion.13
  221.7 0.6 gather_fusion
  222.4 0.7 add_compare_fusion.2
  223.0 1.3 convolution_select_fusion.2
  224.4 3.4 scatter_fusion
  227.8 0.1 compare_select_fusion.13
  227.9 0.6 gather_fusion
  228.6 0.7 add_compare_fusion.2
  229.2 1.3 convolution_select_fusion.2
  230.6 3.4 scatter_fusion
  234.0 0.1 compare_select_fusion.13
  234.1 0.6 gather_fusion
  234.7 0.7 add_compare_fusion.2
  235.4 1.4 convolution_select_fusion.2
  236.8 3.5 %scatter_fusion = f32[32,128,128]{2,1,0:T(8,128)} fusion(f32[32,128,128]{2,1,0:T(8,128)} %get-tuple-element.273, s32[16]{0:T(128)S(1)} %compare_select_fusion.14, f32[16,128,128]{2,1,0:T(8,128)S(1)} %convolution_select_fusion.2), kind=kCustom, calls=%fused_computation.3.clone.1 | custom fusion | flops 262144 | bytes 3145792 | tf_op jit(solution)/shard_map/while/body/eval_jaxpr/scatter-add | solution.py:45
  240.2 0.1 compare_select_fusion.13
  240.3 0.6 gather_fusion
  241.0 0.7 add_compare_fusion.2
  241.6 1.4 convolution_select_fusion.2
  243.0 3.4 scatter_fusion
  246.4 2.8 convert_bitcast_fusion
  249.1 6.5 %all-to-all-start = ((bf16[1,32,128,128]{3,2,0,1:T(8,128)(2,1)}), bf16[1,32,128,128]{3,2,0,1:T(8,128)(2,1)S(1)}, u32[]{:S(2)}, u32[]{:S(2)}) async-start(bf16[1,32,128,128]{3,2,0,1:T(8,128)(2,1)} %convert_bitcast_fusion), calls=%async_computation | async-start | bytes 2097152 | tf_op jit(solution)/shard_map/all_to_all | solution.py:51
  255.7 0.8 copy.44
  256.5 0.8 copy.45
  257.3 23.8 %all-to-all-done = bf16[1,32,128,128]{3,2,0,1:T(8,128)(2,1)S(1)} async-done(((bf16[1,32,128,128]{3,2,0,1:T(8,128)(2,1)}), bf16[1,32,128,128]{3,2,0,1:T(8,128)(2,1)S(1)}, u32[]{:S(2)}, u32[]{:S(2)}) %all-to-all-start) | async-done | bytes 1048608 | tf_op jit(solution)/shard_map/all_to_all | solution.py:51
  281.1 0.1 reduce
  281.3 0.1 copy.39
  281.4 0.7 copy.43
  282.2 54.5 %reduce-scatter.2.cloned.1.call-done = bf16[1,3,128,128]{3,2,1,0:T(8,128)(2,1)} async-done(((bf16[1,96,128,128]{3,2,1,0:T(8,128)(2,1)}), bf16[1,3,128,128]{3,2,1,0:T(8,128)(2,1)}) %reduce-scatter.2.cloned.1.call-update) | async-done | bytes 98320 | tf_op jit(solution)/shard_map/reduce_scatter | solution.py:80
  336.6 1.6 convert_element_type.58
  (23 shorter events, 0.2 us)
Async XLA Ops:
  7.2 70.5 %all-gather.5.cloned.1.call-start = ((), (), s32[]{:S(2)}) async-start(), calls=%async_computation.3 | async-start | bytes 1114112 | tf_op jit(solution)/shard_map/all_gather | solution.py:59
  8.9 170.0 %all-gather.3.cloned.1.call-start = ((), (), s32[]{:S(2)}) async-start(), calls=%async_computation.2 | async-start | bytes 3244032 | tf_op jit(solution)/shard_map/all_gather | solution.py:24
  9.7 326.9 %reduce-scatter.2.cloned.1.call-start = ((), (), s32[]{:S(2)}) async-start(), calls=%async_computation.4 | async-start | bytes 3244032 | tf_op jit(solution)/shard_map/reduce_scatter | solution.py:80
  80.1 98.9 %copy-start = (bf16[96,128,128]{2,1,0:T(8,128)(2,1)}, bf16[96,128,128]{2,1,0:T(8,128)(2,1)S(1)}, u32[]{:S(2)}) copy-start(bf16[96,128,128]{2,1,0:T(8,128)(2,1)S(1)} %gather_fusion.1) | copy-start | bytes 9437188
  185.8 13.1 %copy-start.1 = (bf16[128,896]{0,1:T(8,128)(2,1)S(1)}, bf16[128,896]{0,1:T(8,128)(2,1)}, u32[]{:S(2)}) copy-start(bf16[128,896]{0,1:T(8,128)(2,1)} %copy.36) | copy-start | bytes 688132
  249.1 32.0 %all-to-all-start = ((bf16[1,32,128,128]{3,2,0,1:T(8,128)(2,1)}), bf16[1,32,128,128]{3,2,0,1:T(8,128)(2,1)S(1)}, u32[]{:S(2)}, u32[]{:S(2)}) async-start(bf16[1,32,128,128]{3,2,0,1:T(8,128)(2,1)} %convert_bitcast_fusion), calls=%async_computation | async-start | bytes 2097152 | tf_op jit(solution)/shard_map/all_to_all | solution.py:51
Sparse Core Ops, SparseCore 0:
  10.7 67.0 all-gather.4
  81.1 97.8 all-gather.2
  207.8 128.7 reduce-scatter.1
where the time goes:
time: 351 us; the launch traced here: 345 us
  waiting for transfers between devices  218 us (62%)
  other arithmetic  42.7 us (12%)
  blocking collectives  21.7 us (6%)
  matrix products  20.4 us (6%)
  local copies, waits for them, and re-layouts  20.1 us (6%)
  between operations  15.2 us (4%)
  starting transfers between devices  6.64 us (2%)
    all_gather x1, waiting for transfers between devices, per_device(): lax.all_gather(weight_tiles, 'dp', axis=1, tiled=True)  98.9 us
    reduce_scatter x1, waiting for transfers between devices, per_device(): lax.psum_scatter(grad_buffer.reshape(1, capacity, tile_edge, tile_edge).a...  54.5 us
    all_gather x1, waiting for transfers between devices, per_device(): all_cot = lax.all_gather(cot_local, 'tensor', axis=0, tiled=True)  40 us
    all_to_all x1, waiting for transfers between devices, per_device(): lax.all_to_all(shared, 'tensor', split_axis=1, concat_axis=0, tiled=True)  23.8 us
    squeeze x1, blocking collectives, per_device(): all_slots = fetched_slots[0]  21.7 us
    scatter-add x6, other arithmetic, forward_group(): return totals.at[mod_index].add(product)  20.5 us
    scatter-add x1, other arithmetic, per_device(): hidden_grad = hidden_grad.at[hid_index].add(back)  12.9 us
    unnamed x13, local copies, waits for them, and re-layouts  8.27 us
  transfers between devices with their start and end apart: 4, of which 4 were waited for; matrix products, arithmetic and copies ran while one was open for 15% of the time, Pallas kernels for 0%

commit v1 on v0

v1 whole, which is shorter than its diff:
```python
import jax
import jax.numpy as jnp
from jax import lax
from jax.experimental import pallas as pl
from jax.experimental.pallas import tpu as pltpu
from jax.sharding import PartitionSpec as P

BF = jnp.bfloat16
F32 = jnp.float32
EDGE = 128
MODEL = 32
HID = 7
RING = 8
OWN = 3
SLOTS = 96
SCALE = 4096**-0.5
COPIES = 112
DIRS = (1, -1)


def sigmoid_parts(gate, up):
    gate_val = gate.astype(F32)
    return gate_val, up.astype(F32), jax.nn.sigmoid(gate_val)


def kernel(
    gate_ref, up_ref, cot_ref, w_ref, slot_ref, live_ref,
    proj_ref, gate_out, up_out, tile_out,
    wbuf, cbuf, sbuf, sscal, invv, inv, hid, hid_t, terms, tsib, zrecv, xrecv, pbuf, yrecv, lrecv,
    ssem, rsem, lsem,
):
    d, t = lax.axis_index("dp"), lax.axis_index("tensor")
    z, xh, c = d // 4, (d // 2) % 2, d % 2
    xl, y = t // RING, t % RING
    live = live_ref[0]

    def at(pos, base):
        return lax.rem(pos + base + 2 * RING, RING)

    def on_z(step):
        return {"dp": (at(z, step) * 2 + xh) * 2 + c, "tensor": t}

    def on_y(step):
        return {"dp": d, "tensor": xl * RING + at(y, step)}

    on_x_hi = {"dp": (z * 2 + 1 - xh) * 2 + c, "tensor": t}
    on_core = {"dp": (z * 2 + xh) * 2 + 1 - c, "tensor": t}
    on_x_lo = {"dp": d, "tensor": (1 - xl) * RING + y}

    barrier = pltpu.get_barrier_semaphore()
    near = [on_z(1), on_z(-1), on_y(1), on_y(-1), on_x_hi, on_core, on_x_lo]
    for device in near:
        pl.semaphore_signal(barrier, inc=1, device_id=device, device_id_type=pl.DeviceIdType.MESH)

    copies = {}

    def send(key, src, dst, device):
        n = len(copies)
        copies[key] = pltpu.make_async_remote_copy(
            src_ref=src, dst_ref=dst, send_sem=ssem.at[n], recv_sem=rsem.at[n],
            device_id=device, device_id_type=pl.DeviceIdType.MESH,
        )
        copies[key].start()

    sent = set()

    def drain():
        for key, copy in copies.items():
            if key not in sent:
                copy.wait_send()
                sent.add(key)

    def tiles(pos, part):
        which = xh if part == 0 else 1 - xh
        return wbuf.at[pl.ds((((pos * 2) + which) * 2 + c) * OWN, OWN)]

    def last_hop(way, part):
        return 3 if part == (0 if way == 1 else 1) else 2

    def tile_send(way, k, part, src=None):
        ref = tiles(at(z, -way * k), part)
        send(("A", way, k, part), ref if src is None else src, ref, on_z(way))

    def tile_core(name, pos, part):
        ref = tiles(pos, part)
        send(("AC", name), ref, ref, on_core)

    def tile_event(k, part):
        for way in DIRS:
            if k <= last_hop(way, part):
                copies["A", way, k, part].wait_recv()
                if k + 1 <= last_hop(way, part):
                    tile_send(way, k + 1, part)
        for way in DIRS:
            if k <= last_hop(way, part):
                tile_core((way, k, part), at(z, -way * (k + 1)), part)

    def cols(pos, part):
        which = xl if part == 0 else 1 - xl
        return cbuf.at[pl.ds((which * RING + pos) * 2, 2)]

    def col_send(way, k, part):
        ref = cols(at(y, -way * k), part)
        send(("C", way, k, part), ref, ref, on_y(way))

    def col_event(k, part):
        for way in DIRS:
            if k <= last_hop(way, part):
                copies["C", way, k, part].wait_recv()
                if k + 1 <= last_hop(way, part):
                    col_send(way, k + 1, part)

    def slot_send(way, k):
        ref = sbuf.at[pl.ds(at(z, -way * k) * 4, 4)]
        send(("S", way, k), ref, ref, on_z(way))

    def slot_event(k):
        for way in DIRS:
            if k <= (3 if way == 1 else 2):
                copies["S", way, k].wait_recv()
                if k + 1 <= (3 if way == 1 else 2):
                    slot_send(way, k + 1)

    for half in range(2):
        cbuf[t * 2 + half] = cot_ref[:, half * EDGE : (half + 1) * EDGE]
    lane = lax.broadcasted_iota(jnp.int32, (1, EDGE), 1)
    sbuf[d] = jnp.where(lane == 0, slot_ref[0, 0], jnp.where(lane == 1, slot_ref[0, 1], slot_ref[0, 2]))
    pl.semaphore_wait(barrier, len(near))

    send(("S", "core"), sbuf.at[pl.ds(d, 1)], sbuf.at[pl.ds(d, 1)], on_core)
    own = w_ref.at[0]
    for way in DIRS:
        tile_send(way, 0, 0, own)
        col_send(way, 0, 0)
    send(("C", "x"), cols(y, 0), cols(y, 0), on_x_lo)
    send(("A", "x"), own, tiles(z, 0), on_x_hi)
    send(("AC", "own"), own, tiles(z, 0), on_core)
    wbuf[pl.ds(d * OWN, OWN)] = w_ref[0]
    wbuf[SLOTS] = jnp.zeros((EDGE, EDGE), BF)

    copies["S", "core"].wait_recv()
    pair = sbuf.at[pl.ds((z * 2 + xh) * 2, 2)]
    send(("S", "x"), pair, pair, on_x_hi)

    def hidden_of(h):
        piece = pl.ds(h * EDGE, EDGE) if not isinstance(h, int) else slice(h * EDGE, (h + 1) * EDGE)
        gate_val, up_val, sig = sigmoid_parts(gate_ref[:, piece], up_ref[:, piece])
        value = (gate_val * sig * up_val).astype(BF)
        hid[:, piece] = value
        hid_t[h] = value.T

    for h in range(HID):
        hidden_of(h)

    copies["C", "x"].wait_recv()
    for way in DIRS:
        col_send(way, 0, 1)
    copies["S", "x"].wait_recv()
    for way in DIRS:
        slot_send(way, 0)
    copies["A", "x"].wait_recv()
    for way in DIRS:
        tile_send(way, 0, 1)
    tile_core("x", z, 1)

    col_event(0, 0)
    tile_event(0, 0)
    col_event(0, 1)
    slot_event(0)
    tile_event(0, 1)
    col_event(1, 0)
    slot_event(1)
    col_event(1, 1)
    tile_event(1, 0)
    slot_event(2)
    col_event(2, 0)
    tile_event(1, 1)
    col_event(2, 1)
    slot_event(3)
    to_scalar = pltpu.make_async_copy(sbuf, sscal, lsem.at[0])
    to_scalar.start()
    col_event(3, 0)
    col_event(3, 1)
    to_scalar.wait()

    def quarter(q, core, add):
        def group(i, _):
            owner = (q * 4 + i) * 2 + core
            for j in range(OWN):
                slot = sscal[owner, 0, j]
                factor = jnp.where(owner * OWN + j < live, SCALE, 0.0)
                term = jnp.dot(hid_t[slot // MODEL], cbuf[lax.rem(slot, MODEL)], preferred_element_type=F32) * factor
                if add:
                    term += tsib[(q * 4 + i) * OWN + j].astype(F32)
                terms[core * 48 + (q * 4 + i) * OWN + j] = term.astype(BF)
            return 0

        lax.fori_loop(0, 4, group, 0, unroll=2)

    def for_sibling(q):
        quarter(q, 1 - c, False)
        send(
            ("T", q), terms.at[pl.ds((1 - c) * 48 + q * 12, 12)], tsib.at[pl.ds(q * 12, 12)], on_core
        )

    def for_own(q):
        copies["T", q].wait_recv()
        quarter(q, c, True)

    for_sibling(0)
    for_sibling(1)
    tile_event(2, 0)
    for_sibling(2)
    for_sibling(3)
    tile_event(2, 1)
    for_own(0)
    for_own(1)

    place = lax.broadcasted_iota(jnp.int32, (8, EDGE), 0) * EDGE + lax.broadcasted_iota(jnp.int32, (8, EDGE), 1)

    def invert(i, found):
        for j in range(OWN):
            s = i * OWN + j
            key = jnp.where(s < live, sscal[i, 0, j], -1)
            found = jnp.where(place == key, s, found)
        return found

    invv[...] = lax.fori_loop(0, SLOTS // OWN, invert, jnp.full((8, EDGE), SLOTS, jnp.int32), unroll=4)
    to_inv = pltpu.make_async_copy(invv, inv, lsem.at[1])
    to_inv.start()
    tile_event(3, 0)
    for_own(2)
    for_own(3)
    tile_event(3, 1)

    def first_hop(way, part):
        return 3 - last_hop(way, part)

    def z_local(pos, part):
        which = xh if part == 0 else 1 - xh
        return pl.ds(c * 48 + (pos * 2 + 1 - which) * OWN, OWN)

    def y_local(pos, part):
        which = xl if part == 0 else 1 - xl
        return pl.ds(((1 - which) * RING + pos) * 2, 2)

    rings = {
        "D": (terms, zrecv, z_local, z, on_z),
        "B": (pbuf, yrecv, y_local, y, on_y),
    }

    def ring_send(name, way, k, part, fresh=False):
        local, recv, index, pos, to = rings[name]
        side = 0 if way == 1 else 1
        src = local.at[index(at(pos, way * 4), part)] if k == 0 else recv.at[side, k - 1, part]
        if fresh and k:
            src = local.at[index(at(pos, way * (4 - k)), part)]
        send((name, way, k, part), src, recv.at[side, k, part], to(way))

    def ring_start(name):
        for way in DIRS:
            part = 0 if way == 1 else 1
            ring_send(name, way, 0, part, True)
        for way in DIRS:
            part = 1 if way == 1 else 0
            ring_send(name, way, 1, part, True)

    def ring_event(name, n):
        local, recv, index, pos, to = rings[name]
        for way in DIRS:
            lead = 0 if way == 1 else 1
            part = lead if n % 2 == 0 else 1 - lead
            k = (n + 1) // 2
            side = 0 if way == 1 else 1
            copies[name, way, k, part].wait_recv()
            if k < 3:
                here = index(at(pos, way * (3 - k)), part)
                recv[side, k, part] = (recv[side, k, part].astype(F32) + local[here].astype(F32)).astype(BF)
                ring_send(name, way, k + 1, part)

    def ring_total(name, part):
        local, recv, index, pos, _ = rings[name]
        return (
            recv[0, 3, part].astype(F32) + recv[1, 3, part].astype(F32) + local[index(pos, part)].astype(F32)
        )

    ring_start("D")
    for key in copies:
        if key[0] == "AC":
            copies[key].wait_recv()
    to_inv.wait()

    def weight(h, m):
        p = h * MODEL + m
        return wbuf[inv[p // EDGE, lax.rem(p, EDGE)]]

    def panel(h, m, rows):
        return jnp.concatenate(
            [jnp.concatenate([weight(h + i, m), weight(h + i, m + 1)], axis=1) for i in range(rows)], axis=0
        )

    def forward(who):
        m = who * 2
        total = jnp.dot(hid[:, 6 * EDGE :], panel(6, m, 1), preferred_element_type=F32)
        for h in (0, 2, 4):
            total += jnp.dot(hid[:, h * EDGE : (h + 2) * EDGE], panel(h, m, 2), preferred_element_type=F32)
        pbuf[m] = total[:, :EDGE].astype(BF)
        pbuf[m + 1] = total[:, EDGE:].astype(BF)

    def forward_of(step, part):
        which = xl if part == 0 else 1 - xl
        forward((1 - which) * RING + at(y, step))

    forward_of(4, 0)
    forward_of(4, 1)
    forward_of(3, 1)
    forward_of(-3, 0)
    ring_start("B")
    forward_of(3, 0)
    forward_of(-3, 1)

    def rest(i, _):
        step = jnp.where(i == 4, 0, (2 - i // 2) * (1 - 2 * lax.rem(i, 2)))
        forward_of(step, 0)
        forward_of(step, 1)
        return 0

    lax.fori_loop(0, 5, rest, 0)

    def backward(h, rows):
        def columns(i, total):
            m = i * 2
            left = jnp.concatenate([cbuf[m], cbuf[m + 1]], axis=1)
            return total + lax.dot_general(
                left, panel(h, m, rows), (((1,), (1,)), ((), ())), preferred_element_type=F32
            )

        grad = lax.fori_loop(0, MODEL // 2, columns, jnp.zeros((EDGE, rows * EDGE), F32), unroll=2)
        piece = slice(h * EDGE, (h + rows) * EDGE)
        gate_val, up_val, sig = sigmoid_parts(gate_ref[:, piece], up_ref[:, piece])
        gate_out[:, piece] = (grad * up_val * sig * (1.0 + gate_val * (1.0 - sig))).astype(BF)
        up_out[:, piece] = (grad * (gate_val * sig)).astype(BF)

    ring_event("D", 0)
    ring_event("B", 0)
    ring_event("B", 1)
    ring_event("D", 1)
    ring_event("B", 2)
    ring_event("D", 2)
    ring_event("B", 3)
    ring_event("B", 4)
    ring_event("D", 3)
    ring_event("B", 5)
    ring_event("D", 4)
    ring_event("B", 6)
    there = y_local(y, 0)
    pbuf[there] = ring_total("B", 0).astype(BF)
    send(("B", "x"), pbuf.at[there], lrecv, on_x_lo)
    backward(0, 2)
    ring_event("D", 5)
    backward(2, 2)
    copies["B", "x"].wait_recv()
    whole = ring_total("B", 1) + lrecv[...].astype(F32)
    for half in range(2):
        proj_ref[:, half * EDGE : (half + 1) * EDGE] = whole[half].astype(BF)
    ring_event("D", 6)
    there = z_local(z, 0)
    terms[there] = ring_total("D", 0).astype(BF)
    send(("D", "x"), terms.at[there], xrecv, on_x_hi)
    backward(4, 2)
    backward(6, 1)
    drain()
    copies["D", "x"].wait_recv()
    tile_out[0] = ring_total("D", 1) + xrecv[...].astype(F32)


def per_device(gate_pre, up_pre, cotangent, weight_tiles, tile_slots, live_counts):
    vmem = pl.BlockSpec(memory_space=pltpu.VMEM)
    smem = pl.BlockSpec(memory_space=pltpu.SMEM)
    tile = (EDGE, EDGE)
    return pl.pallas_call(
        kernel,
        out_shape=(
            jax.ShapeDtypeStruct(cotangent.shape, BF),
            jax.ShapeDtypeStruct(gate_pre.shape, BF),
            jax.ShapeDtypeStruct(up_pre.shape, BF),
            jax.ShapeDtypeStruct(weight_tiles.shape, F32),
        ),
        in_specs=[vmem] * 4 + [smem] * 2,
        out_specs=(vmem,) * 4,
        scratch_shapes=[
            pltpu.VMEM((SLOTS + 1, *tile), BF),
            pltpu.VMEM((MODEL, *tile), BF),
            pltpu.VMEM((SLOTS // OWN, 1, EDGE), jnp.int32),
            pltpu.SMEM((SLOTS // OWN, 1, EDGE), jnp.int32),
            pltpu.VMEM((8, EDGE), jnp.int32),
            pltpu.SMEM((8, EDGE), jnp.int32),
            pltpu.VMEM((EDGE, HID * EDGE), BF),
            pltpu.VMEM((HID, *tile), BF),
            pltpu.VMEM((SLOTS, *tile), BF),
            pltpu.VMEM((SLOTS // 2, *tile), BF),
            pltpu.VMEM((2, 4, 2, OWN, *tile), BF),
            pltpu.VMEM((OWN, *tile), BF),
            pltpu.VMEM((MODEL, *tile), BF),
            pltpu.VMEM((2, 4, 2, 2, *tile), BF),
            pltpu.VMEM((2, *tile), BF),
            pltpu.SemaphoreType.DMA((COPIES,)),
            pltpu.SemaphoreType.DMA((COPIES,)),
            pltpu.SemaphoreType.DMA((2,)),
        ],
        compiler_params=pltpu.CompilerParams(
            collective_id=0, has_side_effects=True, vmem_limit_bytes=40 << 20
        ),
    )(gate_pre, up_pre, cotangent, weight_tiles, tile_slots, live_counts)


def solution(mesh):
    in_specs = (
        P("dp", "tensor"),
        P("dp", "tensor"),
        P("dp", "tensor"),
        P("tensor", "dp", None, None),
        P("tensor", "dp"),
        P("tensor"),
    )
    out_specs = (
        P("dp", "tensor"),
        P("dp", "tensor"),
        P("dp", "tensor"),
        P("tensor", "dp", None, None),
    )
    return jax.shard_map(
        per_device, mesh=mesh, in_specs=in_specs, out_specs=out_specs, check_vma=False
    )
```

time: 351 us -> 74.3 us (0.21); the launches traced: 345 us -> 73.6 us
  waiting for transfers between devices: 218 us -> 0 us
  Pallas kernels: 0 us -> 66 us
  other arithmetic: 42.7 us -> 0 us
  blocking collectives: 21.7 us -> 0 us
  matrix products: 20.4 us -> 0 us
  between operations: 15.2 us -> 1.33 us
  local copies, waits for them, and re-layouts: 20.1 us -> 6.29 us
  starting transfers between devices: 6.64 us -> 0 us
    all_gather x2 -> x0, waiting for transfers between devices: 139 us -> none  [the longest x1 98.9 us: per_device(): lax.all_gather(weight_tiles, 'dp', axis=1, tiled=True)]
    pallas_call x0 -> x1, Pallas kernels: none -> 66 us  [per_device(): pl.pallas_call(kernel, out_shape=(jax.ShapeDtypeStruct(cotangent.shape, B...]
    reduce_scatter x1 -> x0, waiting for transfers between devices: 54.5 us -> none  [per_device(): lax.psum_scatter(grad_buffer.reshape(1, capacity, tile_edge, tile_edge).a...]
    scatter-add x7 -> x0, other arithmetic: 33.4 us -> none  [the longest x6 20.5 us: forward_group(): return totals.at[mod_index].add(product)]
    all_to_all x1 -> x0, waiting for transfers between devices: 23.8 us -> none  [per_device(): lax.all_to_all(shared, 'tensor', split_axis=1, concat_axis=0, tiled=True)]
    squeeze x1 -> x0, blocking collectives: 21.7 us -> none  [per_device(): all_slots = fetched_slots[0]]
    dot_general x8 -> x0, matrix products: 20.4 us -> none  [the longest x6 8.09 us: forward_group(): jnp.einsum('gtb,gbc->gtc', picked, group_tiles, preferred_element_type=jn...]
    gather x8 -> x0, local copies, waits for them, and re-layouts: 8.98 us -> none  [the longest x6 3.87 us: forward_group(): picked = hidden_blocks[hid_index]]
  transfers between devices with their start and end apart: 4 -> 0, of which waited for: 4 -> 0; matrix products, arithmetic and copies ran while one was open for 15% -> 0% of each run, Pallas kernels for 0% -> 0%
where the time goes in v1:
time: 74.3 us; the launch traced here: 73.6 us
  Pallas kernels  66 us (89%)
  local copies, waits for them, and re-layouts  6.29 us (8%)
  between operations  1.33 us (2%)
    pallas_call x1, Pallas kernels, per_device(): pl.pallas_call(kernel, out_shape=(jax.ShapeDtypeStruct(cotangent.shape, B...  66 us
    unnamed x14, local copies, waits for them, and re-layouts  6.29 us

profile of v1, /device:TPU:1, one launch (start us, length us, event | category | flops | bytes accessed | tf_op | source)
XLA Modules:
  0.0 73.6 jit_solution(3056924321464058656)
XLA Ops:
  0.6 0.0 copy-start.4
  1.3 0.0 copy-done.4
  1.3 0.0 copy-start
  1.3 0.9 %copy-done = bf16[128,896]{1,0:T(8,128)(2,1)S(1)} copy-done((bf16[128,896]{1,0:T(8,128)(2,1)S(1)}, bf16[128,896]{1,0:T(8,128)(2,1)}, u32[]{:S(2)}) %copy-start) | copy-done | bytes 229400
  2.3 0.0 copy-start.1
  2.3 0.9 %copy-done.1 = bf16[128,896]{1,0:T(8,128)(2,1)S(1)} copy-done((bf16[128,896]{1,0:T(8,128)(2,1)S(1)}, bf16[128,896]{1,0:T(8,128)(2,1)}, u32[]{:S(2)}) %copy-start.1) | copy-done | bytes 229400
  3.2 0.0 copy-start.2
  3.2 0.9 %copy-done.2 = bf16[1,3,128,128]{3,2,1,0:T(8,128)(2,1)S(1)} copy-done((bf16[1,3,128,128]{3,2,1,0:T(8,128)(2,1)S(1)}, bf16[1,3,128,128]{3,2,1,0:T(8,128)(2,1)}, u32[]{:S(2)}) %copy-start.2) | copy-done | bytes 98328
  4.1 0.0 copy-start.3
  4.1 0.8 %copy-done.3 = bf16[128,256]{1,0:T(8,128)(2,1)S(1)} copy-done((bf16[128,256]{1,0:T(8,128)(2,1)S(1)}, bf16[128,256]{1,0:T(8,128)(2,1)}, u32[]{:S(2)}) %copy-start.3) | copy-done | bytes 65560
  4.9 66.0 %shard_map.93 = (bf16[128,256]{1,0:T(8,128)(2,1)S(1)}, bf16[128,896]{1,0:T(8,128)(2,1)S(1)}, bf16[128,896]{1,0:T(8,128)(2,1)S(1)}, f32[1,3,128,128]{3,2,1,0:T(8,128)S(1)}) custom-call(bf16[128,896]{1,0:T(8,128)(2,1)S(1)} %copy-done, bf16[128,896]{1,0:T(8,128)(2,1)S(1)} %copy-done.1, bf16[128,256]{1,0:T(8,128)(2,1)S(1)} %copy-done.3, ...), custom_call_target="tpu_custom_call" | custom-call | tf_op jit(solution)/shard_map/pallas_call | solution.py:381
  70.9 0.6 copy.15
  71.6 0.7 copy.16
  72.2 0.7 copy.17
  72.9 0.7 copy.18
Async XLA Ops:
  0.6 0.7 copy-start.4
  1.3 0.9 %copy-start = (bf16[128,896]{1,0:T(8,128)(2,1)S(1)}, bf16[128,896]{1,0:T(8,128)(2,1)}, u32[]{:S(2)}) copy-start(bf16[128,896]{1,0:T(8,128)(2,1)} %gate_ref.1) | copy-start | bytes 688132
  2.3 0.9 %copy-start.1 = (bf16[128,896]{1,0:T(8,128)(2,1)S(1)}, bf16[128,896]{1,0:T(8,128)(2,1)}, u32[]{:S(2)}) copy-start(bf16[128,896]{1,0:T(8,128)(2,1)} %up_ref.1) | copy-start | bytes 688132
  3.2 0.9 %copy-start.2 = (bf16[1,3,128,128]{3,2,1,0:T(8,128)(2,1)S(1)}, bf16[1,3,128,128]{3,2,1,0:T(8,128)(2,1)}, u32[]{:S(2)}) copy-start(bf16[1,3,128,128]{3,2,1,0:T(8,128)(2,1)} %w_ref.1) | copy-start | bytes 294916
  4.1 0.8 %copy-start.3 = (bf16[128,256]{1,0:T(8,128)(2,1)S(1)}, bf16[128,256]{1,0:T(8,128)(2,1)}, u32[]{:S(2)}) copy-start(bf16[128,256]{1,0:T(8,128)(2,1)} %cot_ref.1) | copy-start | bytes 196612

commit v2 on v0

v2 whole, which is shorter than its diff:
```python
import math

import jax
import jax.numpy as jnp
from jax import lax
from jax.experimental import pallas as pl
from jax.experimental.pallas import tpu as pltpu
from jax.sharding import PartitionSpec as P

BF = jnp.bfloat16
F32 = jnp.float32
EDGE = 128
MODEL = 32
HID = 7
RING = 8
OWN = 3
SLOTS = 96
SCALE = 4096**-0.5
DIRS = (1, -1)
FAR_FIRST = (4, 3, 5, 2, 6, 1, 7, 0)
VMEM_BYTES = 62 << 20
SEND_SEMS, RECV_SEMS = 7, 84


def sigmoid_parts(gate, up):
    gate_val = gate.astype(F32)
    return gate_val, up.astype(F32), jax.nn.sigmoid(gate_val)


class Traffic:
    def __init__(self, send_sems, recv_sems):
        self.send_sems, self.recv_sems = send_sems, recv_sems
        self.leaving, self.coming = {}, {}
        self.ids = {}

    def sem(self, sems, kind, key):
        ids = self.ids.setdefault(kind, {})
        return sems.at[ids.setdefault(key, len(ids))]

    def send(self, family, key, src, dst, device):
        copy = pltpu.make_async_remote_copy(
            src_ref=src,
            dst_ref=dst,
            send_sem=self.sem(self.send_sems, "leave", family),
            recv_sem=self.sem(self.recv_sems, "come", (family, key)),
            device_id=device,
            device_id_type=pl.DeviceIdType.MESH,
        )
        copy.start()
        self.leaving.setdefault(family, []).append((copy, math.prod(src.shape)))
        self.coming.setdefault((family, key), []).append((copy, math.prod(dst.shape), device))

    def arrive(self, family, key, like):
        copies = self.coming.pop((family, key))
        assert sum(c[1] for c in copies) == math.prod(like.shape)
        sem = self.sem(self.recv_sems, "come", (family, key))
        pltpu.make_async_remote_copy(
            src_ref=like, dst_ref=like, send_sem=sem, recv_sem=sem,
            device_id=copies[0][2], device_id_type=pl.DeviceIdType.MESH,
        ).wait_recv()

    def left(self, family, like):
        copies = self.leaving.pop(family)
        assert sum(c[1] for c in copies) == math.prod(like.shape)
        sem = self.sem(self.send_sems, "leave", family)
        pltpu.make_async_remote_copy(
            src_ref=like, dst_ref=like, send_sem=sem, recv_sem=sem,
            device_id=self.coming_device, device_id_type=pl.DeviceIdType.MESH,
        ).wait_send()


def kernel(
    gate_hbm, up_hbm, cot_hbm, w_hbm, slot_ref, live_ref,
    proj_hbm, gate_out_hbm, up_out_hbm, tile_hbm,
    proj_ref, gate_out, up_out, tile_out, gate_ref, up_ref, wbuf, cbuf, sbuf, sscal, invv, inv, hid, hid_t, terms, tsib, zrecv, xrecv, pbuf, yrecv, lrecv,
    ssem, rsem, lsem,
):
    d, t = lax.axis_index("dp"), lax.axis_index("tensor")
    z, xh, c = d // 4, (d // 2) % 2, d % 2
    xl, y = t // RING, t % RING

    def at(pos, base):
        return lax.rem(pos + base + 2 * RING, RING)

    def on_z(step):
        return {"dp": (at(z, step) * 2 + xh) * 2 + c, "tensor": t}

    def on_y(step):
        return {"dp": d, "tensor": xl * RING + at(y, step)}

    on_x_hi = {"dp": (z * 2 + 1 - xh) * 2 + c, "tensor": t}
    on_core = {"dp": (z * 2 + xh) * 2 + 1 - c, "tensor": t}
    on_x_lo = {"dp": d, "tensor": (1 - xl) * RING + y}

    loads = [
        pltpu.make_async_copy(w_hbm.at[0], wbuf.at[pl.ds(d * OWN, OWN)], lsem.at[0]),
        pltpu.make_async_copy(cot_hbm.at[:, pl.ds(0, EDGE)], cbuf.at[t * 2], lsem.at[1]),
        pltpu.make_async_copy(cot_hbm.at[:, pl.ds(EDGE, EDGE)], cbuf.at[t * 2 + 1], lsem.at[2]),
        pltpu.make_async_copy(gate_hbm, gate_ref, lsem.at[3]),
        pltpu.make_async_copy(up_hbm, up_ref, lsem.at[4]),
    ]
    for load in loads:
        load.start()

    barrier = pltpu.get_barrier_semaphore()
    near = [on_z(i) for i in range(1, RING)] + [on_y(1), on_y(-1), on_x_hi, on_core, on_x_lo]
    for device in near:
        pl.semaphore_signal(barrier, inc=1, device_id=device, device_id_type=pl.DeviceIdType.MESH)

    live = live_ref[0]
    traffic = Traffic(ssem, rsem)
    traffic.coming_device = on_core

    def tiles(pos, part, first=0, count=OWN):
        which = xh if part == 0 else 1 - xh
        return wbuf.at[pl.ds((((pos * 2) + which) * 2 + c) * OWN + first, count)]

    def last_hop(way, part):
        return 3 if part == (0 if way == 1 else 1) else 2

    def ways_of(k, part):
        return [way for way in DIRS if k <= last_hop(way, part)]

    def tile_send(way, k, part, i):
        ref = tiles(at(z, -way * k), part, i, 1)
        traffic.send("A", (k, part, i), ref, ref, on_z(way))

    def tile_core(pos, part):
        ref = tiles(pos, part)
        traffic.send("K", 0, ref, ref, on_core)

    def tile_event(k, part, i):
        ways = ways_of(k, part)
        traffic.arrive("A", (k, part, i), wbuf.at[pl.ds(0, len(ways))])
        for way in ways_of(k + 1, part):
            tile_send(way, k + 1, part, i)
        if i == OWN - 1:
            for way in ways:
                tile_core(at(z, -way * (k + 1)), part)

    def tile_x_event(i):
        traffic.arrive("A", ("x", i), wbuf.at[pl.ds(0, 1)])
        for way in DIRS:
            tile_send(way, 0, 1, i)
        if i == OWN - 1:
            tile_core(z, 1)

    def column(pos, part, i):
        which = xl if part == 0 else 1 - xl
        return cbuf.at[pl.ds((which * RING + pos) * 2 + i, 1)]

    def col_send(way, k, part, i):
        ref = column(at(y, -way * k), part, i)
        traffic.send("C", (k, part, i), ref, ref, on_y(way))

    def col_event(k, part, i):
        traffic.arrive("C", (k, part, i), cbuf.at[pl.ds(0, len(ways_of(k, part)))])
        for way in ways_of(k + 1, part):
            col_send(way, k + 1, part, i)

    def col_x_event(i):
        traffic.arrive("C", ("x", i), cbuf.at[pl.ds(0, 1)])
        for way in DIRS:
            col_send(way, 0, 1, i)

    def rows(first, count):
        return sbuf.at[pl.ds(first, count)]

    def row_z_event():
        traffic.arrive("S", "z", rows(0, RING - 1))
        ref = rows((c * 2 + xh) * RING, RING)
        traffic.send("S", "x", ref, ref, on_x_hi)

    def row_x_event():
        traffic.arrive("S", "x", rows(0, RING))
        ref = rows(c * 2 * RING, 2 * RING)
        traffic.send("S", "core", ref, ref, on_core)

    lane = lax.broadcasted_iota(jnp.int32, (1, EDGE), 1)
    mine = (c * 2 + xh) * RING + z
    sbuf[mine] = jnp.where(lane == 0, slot_ref[0, 0], jnp.where(lane == 1, slot_ref[0, 1], slot_ref[0, 2]))
    wbuf[SLOTS] = jnp.zeros((EDGE, EDGE), BF)
    loads[0].wait()
    pl.semaphore_wait(barrier, len(near))

    for i in range(1, RING):
        traffic.send("S", "z", rows(mine, 1), rows(mine, 1), on_z(i))
    for i in range(OWN):
        ref = tiles(z, 0, i, 1)
        traffic.send("A", ("x", i), ref, ref, on_x_hi)
        for way in DIRS:
            tile_send(way, 0, 0, i)
    loads[1].wait()
    loads[2].wait()
    for i in range(2):
        ref = column(y, 0, i)
        traffic.send("C", ("x", i), ref, ref, on_x_lo)
        for way in DIRS:
            col_send(way, 0, 0, i)
    tile_core(z, 0)
    loads[3].wait()
    loads[4].wait()

    def hidden_of(h):
        piece = slice(h * EDGE, (h + 1) * EDGE)
        gate_val, up_val, sig = sigmoid_parts(gate_ref[:, piece], up_ref[:, piece])
        value = (gate_val * sig * up_val).astype(BF)
        hid[:, piece] = value
        hid_t[h] = value.T

    for h in range(HID):
        hidden_of(h)

    tile_event(0, 0, 0)
    col_event(0, 0, 0)
    col_x_event(0)
    tile_event(0, 0, 1)
    col_event(0, 0, 1)
    col_x_event(1)
    tile_x_event(0)
    tile_event(0, 0, 2)
    row_z_event()
    tile_x_event(1)
    tile_x_event(2)
    tile_event(1, 0, 0)
    col_event(1, 0, 0)
    col_event(0, 1, 0)
    tile_event(1, 0, 1)
    col_event(1, 0, 1)
    tile_event(0, 1, 0)
    row_x_event()
    col_event(0, 1, 1)
    tile_event(1, 0, 2)
    tile_event(0, 1, 1)
    col_event(2, 0, 0)
    tile_event(0, 1, 2)
    col_event(1, 1, 0)
    traffic.arrive("S", "core", rows(0, 2 * RING))
    to_scalar = pltpu.make_async_copy(sbuf, sscal, lsem.at[0])
    to_scalar.start()
    col_event(2, 0, 1)
    tile_event(2, 0, 0)
    col_event(1, 1, 1)
    tile_event(2, 0, 1)
    col_event(3, 0, 0)
    tile_event(1, 1, 0)
    col_event(2, 1, 0)
    tile_event(2, 0, 2)
    to_scalar.wait()

    def row_of(owner_z, owner_x, owner_core):
        return (owner_core * 2 + owner_x) * RING + owner_z

    place = lax.broadcasted_iota(jnp.int32, (8, EDGE), 0) * EDGE + lax.broadcasted_iota(jnp.int32, (8, EDGE), 1)

    def invert(i, found):
        row = row_of(i // 4, lax.rem(i // 2, 2), lax.rem(i, 2))
        for j in range(OWN):
            s = i * OWN + j
            key = jnp.where(s < live, sscal[row, 0, j], -1)
            found = jnp.where(place == key, s, found)
        return found

    invv[...] = lax.fori_loop(0, SLOTS // OWN, invert, jnp.full((8, EDGE), SLOTS, jnp.int32), unroll=4)
    to_inv = pltpu.make_async_copy(invv, inv, lsem.at[1])
    to_inv.start()

    col_event(3, 0, 1)
    tile_event(1, 1, 1)
    col_event(2, 1, 1)
    tile_event(1, 1, 2)
    tile_event(3, 0, 0)
    col_event(3, 1, 0)
    col_event(3, 1, 1)

    def group(owner_z, core, add):
        for owner_x in range(2):
            row = row_of(owner_z, owner_x, core)
            for j in range(OWN):
                slot = sscal[row, 0, j]
                s = ((owner_z * 2 + owner_x) * 2 + core) * OWN + j
                factor = jnp.where(s < live, SCALE, 0.0)
                term = jnp.dot(hid_t[slot // MODEL], cbuf[lax.rem(slot, MODEL)], preferred_element_type=F32) * factor
                index = (owner_z * 2 + owner_x) * OWN + j
                if add:
                    term += tsib[index].astype(F32)
                terms[core * 48 + index] = term.astype(BF)

    def for_sibling(n):
        owner_z = at(z, FAR_FIRST[n])
        group(owner_z, 1 - c, False)
        traffic.send(
            "T", n, terms.at[pl.ds((1 - c) * 48 + owner_z * 6, 6)], tsib.at[pl.ds(owner_z * 6, 6)], on_core
        )

    def for_own(n):
        traffic.arrive("T", n, tsib.at[pl.ds(0, 6)])
        group(at(z, FAR_FIRST[n]), c, True)

    def z_local(pos, part):
        which = 1 - xh if part == 0 else xh
        return pl.ds(c * 48 + (pos * 2 + which) * OWN, OWN)

    def y_local(pos, part, i):
        which = 1 - xl if part == 0 else xl
        return pl.ds((which * RING + pos) * 2 + i, 1)

    def y_fresh(way, k, part):
        side = 0 if way == 1 else 1
        for i in range(2):
            src = pbuf.at[y_local(at(y, way * (4 - k)), part, i)]
            traffic.send("B", (k, part if way == 1 else 1 - part, i), src, yrecv.at[side, k, part, pl.ds(i, 1)], on_y(way))

    def z_key(way, k, part):
        return (k, part if way == 1 else 1 - part)

    def z_start():
        for k in range(2):
            for way in DIRS:
                part = k if way == 1 else 1 - k
                src = terms.at[z_local(at(z, way * (4 - k)), part)]
                side = 0 if way == 1 else 1
                traffic.send("D", z_key(way, k, part), src, zrecv.at[side, k, part], on_z(way))

    def z_event(n):
        k, lead = (n + 1) // 2, n % 2
        traffic.arrive("D", (k, lead), terms.at[pl.ds(0, 2 * OWN)])
        for way in DIRS:
            part = lead if way == 1 else 1 - lead
            side = 0 if way == 1 else 1
            if k < 3:
                here = z_local(at(z, way * (3 - k)), part)
                zrecv[side, k, part] = (zrecv[side, k, part].astype(F32) + terms[here].astype(F32)).astype(BF)
                traffic.send(
                    "D", z_key(way, k + 1, part), zrecv.at[side, k, part], zrecv.at[side, k + 1, part], on_z(way)
                )

    def z_total(part):
        return (
            zrecv[0, 3, part].astype(F32) + zrecv[1, 3, part].astype(F32) + terms[z_local(z, part)].astype(F32)
        )

    def y_start(k):
        for way in DIRS:
            y_fresh(way, k, k if way == 1 else 1 - k)

    def y_event(n, i):
        k, lead = (n + 1) // 2, n % 2
        traffic.arrive("B", (k, lead, i), pbuf.at[pl.ds(0, 2)])
        for way in DIRS:
            part = lead if way == 1 else 1 - lead
            side = 0 if way == 1 else 1
            if k < 3:
                here = y_local(at(y, way * (3 - k)), part, i)
                held = yrecv.at[side, k, part, pl.ds(i, 1)]
                held[...] = (held[...].astype(F32) + pbuf[here].astype(F32)).astype(BF)
                traffic.send("B", (k + 1, lead, i), held, yrecv.at[side, k + 1, part, pl.ds(i, 1)], on_y(way))

    def y_total(part, i):
        return (
            yrecv[0, 3, part, i].astype(F32) + yrecv[1, 3, part, i].astype(F32)
            + pbuf[y_local(y, part, i)][0].astype(F32)
        )

    for_sibling(0)
    for_sibling(1)
    for_sibling(2)
    tile_event(3, 0, 1)
    tile_event(2, 1, 0)
    for_own(0)
    for_own(1)
    for_own(2)
    tile_event(3, 0, 2)
    tile_event(2, 1, 1)
    tile_event(2, 1, 2)
    z_start()
    for n in range(3, 8):
        for_sibling(n)
    tile_event(3, 1, 0)
    tile_event(3, 1, 1)
    tile_event(3, 1, 2)
    for n in range(3, 6):
        for_own(n)
    to_inv.wait()
    traffic.arrive("K", 0, wbuf.at[pl.ds(0, 48)])

    def weight(h, m):
        p = h * MODEL + m
        return wbuf[inv[p // EDGE, lax.rem(p, EDGE)]]

    def panel(h, m, count):
        return jnp.concatenate(
            [jnp.concatenate([weight(h + i, m), weight(h + i, m + 1)], axis=1) for i in range(count)], axis=0
        )

    def forward_of(step, part):
        which = 1 - xl if part == 0 else xl
        m = (which * RING + at(y, step)) * 2
        total = jnp.dot(hid[:, 6 * EDGE :], panel(6, m, 1), preferred_element_type=F32)
        for h in (0, 2, 4):
            total += jnp.dot(hid[:, h * EDGE : (h + 2) * EDGE], panel(h, m, 2), preferred_element_type=F32)
        pbuf[m] = total[:, :EDGE].astype(BF)
        pbuf[m + 1] = total[:, EDGE:].astype(BF)

    def backward(h, count):
        def columns(i, total):
            m = i * 2
            left = jnp.concatenate([cbuf[m], cbuf[m + 1]], axis=1)
            return total + lax.dot_general(
                left, panel(h, m, count), (((1,), (1,)), ((), ())), preferred_element_type=F32
            )

        grad = lax.fori_loop(0, MODEL // 2, columns, jnp.zeros((EDGE, count * EDGE), F32), unroll=2)
        piece = slice(h * EDGE, (h + count) * EDGE)
        gate_val, up_val, sig = sigmoid_parts(gate_ref[:, piece], up_ref[:, piece])
        gate_out[:, piece] = (grad * up_val * sig * (1.0 + gate_val * (1.0 - sig))).astype(BF)
        up_out[:, piece] = (grad * (gate_val * sig)).astype(BF)

    forward_of(4, 0)
    forward_of(4, 1)
    y_start(0)
    forward_of(3, 1)
    forward_of(-3, 0)
    y_start(1)
    z_event(0)
    for_own(6)
    for_own(7)
    forward_of(3, 0)
    forward_of(-3, 1)

    def rest(i, _):
        step = (2 - i // 2) * (1 - 2 * lax.rem(i, 2))
        forward_of(step, 0)
        forward_of(step, 1)
        return 0

    lax.fori_loop(0, 4, rest, 0)
    z_event(1)
    y_event(0, 0)
    y_event(0, 1)
    y_event(1, 0)
    y_event(1, 1)
    forward_of(0, 0)
    forward_of(0, 1)
    z_event(2)
    y_event(2, 0)
    y_event(2, 1)
    y_event(3, 0)
    z_event(3)
    y_event(3, 1)
    y_event(4, 0)
    y_event(4, 1)
    z_event(4)
    y_event(5, 0)
    y_event(5, 1)
    backward(0, 2)
    z_event(5)
    for i in range(2):
        y_event(6, i)
        there = y_local(y, 0, i)
        pbuf[there] = y_total(0, i).astype(BF)[None]
        traffic.send("B", ("x", i), pbuf.at[there], lrecv.at[pl.ds(i, 1)], on_x_lo)
    backward(2, 2)
    z_event(6)
    there = z_local(z, 0)
    terms[there] = z_total(0).astype(BF)
    traffic.send("D", "x", terms.at[there], xrecv, on_x_hi)
    backward(4, 2)
    backward(6, 1)
    for i in range(2):
        traffic.arrive("B", ("x", i), lrecv.at[pl.ds(0, 1)])
        proj_ref[:, i * EDGE : (i + 1) * EDGE] = (y_total(1, i) + lrecv[i].astype(F32)).astype(BF)
    stores = [
        pltpu.make_async_copy(gate_out, gate_out_hbm, lsem.at[0]),
        pltpu.make_async_copy(up_out, up_out_hbm, lsem.at[1]),
        pltpu.make_async_copy(proj_ref, proj_hbm, lsem.at[2]),
        pltpu.make_async_copy(tile_out, tile_hbm, lsem.at[3]),
    ]
    for store in stores[:3]:
        store.start()
    traffic.left("S", rows(0, 7 + 8 + 16))
    traffic.left("A", wbuf.at[pl.ds(0, 45)])
    traffic.left("K", wbuf.at[pl.ds(0, 48)])
    traffic.left("C", cbuf.at[pl.ds(0, 30)])
    traffic.left("T", tsib.at[pl.ds(0, 48)])
    traffic.left("B", pbuf.at[pl.ds(0, 30)])
    traffic.arrive("D", "x", xrecv)
    tile_out[0] = z_total(1) + xrecv[...].astype(F32)
    stores[3].start()
    traffic.left("D", terms.at[pl.ds(0, 45)])
    for store in stores:
        store.wait()


def hand_out(*refs):
    n = (len(refs) - 1) // 3
    given, out, held, sems = refs[:n], refs[n : 2 * n], refs[2 * n : 3 * n], refs[-1]
    loads = [pltpu.make_async_copy(given[i], held[i], sems.at[0, i]) for i in range(n)]
    stores = [pltpu.make_async_copy(held[i], out[i], sems.at[1, i]) for i in range(n)]
    for load in loads:
        load.start()
    for load, store in zip(loads, stores):
        load.wait()
        store.start()
    for store in stores:
        store.wait()


def per_device(gate_pre, up_pre, cotangent, weight_tiles, tile_slots, live_counts):
    smem = pl.BlockSpec(memory_space=pltpu.SMEM)
    hbm = pl.BlockSpec(memory_space=pl.ANY)
    tile = (EDGE, EDGE)
    shapes = (
        jax.ShapeDtypeStruct(cotangent.shape, BF),
        jax.ShapeDtypeStruct(gate_pre.shape, BF),
        jax.ShapeDtypeStruct(up_pre.shape, BF),
        jax.ShapeDtypeStruct(weight_tiles.shape, F32),
    )
    results = pl.pallas_call(
        kernel,
        out_shape=shapes,
        in_specs=[hbm] * 4 + [smem] * 2,
        out_specs=(hbm,) * 4,
        scratch_shapes=[
            *[pltpu.VMEM(shape.shape, shape.dtype) for shape in shapes],
            pltpu.VMEM(gate_pre.shape, BF),
            pltpu.VMEM(up_pre.shape, BF),
            pltpu.VMEM((SLOTS + 1, *tile), BF),
            pltpu.VMEM((MODEL, *tile), BF),
            pltpu.VMEM((SLOTS // OWN, 1, EDGE), jnp.int32),
            pltpu.SMEM((SLOTS // OWN, 1, EDGE), jnp.int32),
            pltpu.VMEM((8, EDGE), jnp.int32),
            pltpu.SMEM((8, EDGE), jnp.int32),
            pltpu.VMEM((EDGE, HID * EDGE), BF),
            pltpu.VMEM((HID, *tile), BF),
            pltpu.VMEM((SLOTS, *tile), BF),
            pltpu.VMEM((SLOTS // 2, *tile), BF),
            pltpu.VMEM((2, 4, 2, OWN, *tile), BF),
            pltpu.VMEM((OWN, *tile), BF),
            pltpu.VMEM((MODEL, *tile), BF),
            pltpu.VMEM((2, 4, 2, 2, *tile), BF),
            pltpu.VMEM((2, *tile), BF),
            pltpu.SemaphoreType.DMA((SEND_SEMS,)),
            pltpu.SemaphoreType.DMA((RECV_SEMS,)),
            pltpu.SemaphoreType.DMA((5,)),
        ],
        compiler_params=pltpu.CompilerParams(
            collective_id=0, has_side_effects=True, vmem_limit_bytes=VMEM_BYTES
        ),
    )(gate_pre, up_pre, cotangent, weight_tiles, tile_slots, live_counts)
    return pl.pallas_call(
        hand_out,
        out_shape=shapes,
        in_specs=[hbm] * 4,
        out_specs=(hbm,) * 4,
        scratch_shapes=[pltpu.VMEM(shape.shape, shape.dtype) for shape in shapes] + [pltpu.SemaphoreType.DMA((2, 4))],
        compiler_params=pltpu.CompilerParams(vmem_limit_bytes=VMEM_BYTES),
    )(*results)


def solution(mesh):
    in_specs = (
        P("dp", "tensor"),
        P("dp", "tensor"),
        P("dp", "tensor"),
        P("tensor", "dp", None, None),
        P("tensor", "dp"),
        P("tensor"),
    )
    out_specs = (
        P("dp", "tensor"),
        P("dp", "tensor"),
        P("dp", "tensor"),
        P("tensor", "dp", None, None),
    )
    return jax.shard_map(
        per_device, mesh=mesh, in_specs=in_specs, out_specs=out_specs, check_vma=False
    )
```

time: 351 us -> 67.3 us (0.19); the launches traced: 345 us -> 67.1 us
  waiting for transfers between devices: 218 us -> 0 us
  Pallas kernels: 0 us -> 65.8 us
  other arithmetic: 42.7 us -> 0 us
  blocking collectives: 21.7 us -> 0 us
  matrix products: 20.4 us -> 0 us
  local copies, waits for them, and re-layouts: 20.1 us -> 0 us
  between operations: 15.2 us -> 1.29 us
  starting transfers between devices: 6.64 us -> 0 us
    all_gather x2 -> x0, waiting for transfers between devices: 139 us -> none  [the longest x1 98.9 us: per_device(): lax.all_gather(weight_tiles, 'dp', axis=1, tiled=True)]
    pallas_call x0 -> x2, Pallas kernels: none -> 65.8 us  [the longest x1 63.9 us: per_device(): pl.pallas_call(kernel, out_shape=shapes, in_specs=[hbm] * 4 + [smem] * 2,...]
    reduce_scatter x1 -> x0, waiting for transfers between devices: 54.5 us -> none  [per_device(): lax.psum_scatter(grad_buffer.reshape(1, capacity, tile_edge, tile_edge).a...]
    scatter-add x7 -> x0, other arithmetic: 33.4 us -> none  [the longest x6 20.5 us: forward_group(): return totals.at[mod_index].add(product)]
    all_to_all x1 -> x0, waiting for transfers between devices: 23.8 us -> none  [per_device(): lax.all_to_all(shared, 'tensor', split_axis=1, concat_axis=0, tiled=True)]
    squeeze x1 -> x0, blocking collectives: 21.7 us -> none  [per_device(): all_slots = fetched_slots[0]]
    dot_general x8 -> x0, matrix products: 20.4 us -> none  [the longest x6 8.09 us: forward_group(): jnp.einsum('gtb,gbc->gtc', picked, group_tiles, preferred_element_type=jn...]
    gather x8 -> x0, local copies, waits for them, and re-layouts: 8.98 us -> none  [the longest x6 3.87 us: forward_group(): picked = hidden_blocks[hid_index]]
  transfers between devices with their start and end apart: 4 -> 0, of which waited for: 4 -> 0; matrix products, arithmetic and copies ran while one was open for 15% -> 0% of each run, Pallas kernels for 0% -> 0%
where the time goes in v2:
time: 67.3 us; the launch traced here: 67.1 us
  Pallas kernels  65.8 us (98%)
  between operations  1.29 us (2%)
    pallas_call x1, Pallas kernels, per_device(): pl.pallas_call(kernel, out_shape=shapes, in_specs=[hbm] * 4 + [smem] * 2,...  63.9 us
    pallas_call x1, Pallas kernels, per_device(): pl.pallas_call(hand_out, out_shape=shapes, in_specs=[hbm] * 4, out_specs=...  1.93 us

profile of v2, /device:TPU:1, one launch (start us, length us, event | category | flops | bytes accessed | tf_op | source)
XLA Modules:
  0.0 67.1 jit_solution(14157056665505101902)
XLA Ops:
  1.3 63.9 %shard_map.93 = (bf16[128,256]{1,0:T(8,128)(2,1)}, bf16[128,896]{1,0:T(8,128)(2,1)}, bf16[128,896]{1,0:T(8,128)(2,1)}, f32[1,3,128,128]{3,2,1,0:T(8,128)}) custom-call(bf16[128,896]{1,0:T(8,128)(2,1)} %gate_hbm.1, bf16[128,896]{1,0:T(8,128)(2,1)} %up_hbm.1, bf16[128,256]{1,0:T(8,128)(2,1)} %cot_hbm.1, bf16[1,3,128,128]{3,2,1,0:T(8,128)(2,1)} %w_hbm.1, ...), custom_call_target="tpu_custom_call" | custom-call | tf_op jit(solution)/shard_map/pallas_call | solution.py:519
  65.1 1.9 %shard_map.94 = (bf16[128,256]{1,0:T(8,128)(2,1)}, bf16[128,896]{1,0:T(8,128)(2,1)}, bf16[128,896]{1,0:T(8,128)(2,1)}, f32[1,3,128,128]{3,2,1,0:T(8,128)}) custom-call(bf16[128,256]{1,0:T(8,128)(2,1)} %get-tuple-element.8.refs_0_, bf16[128,896]{1,0:T(8,128)(2,1)} %get-tuple-element.9.refs_1_, bf16[128,896]{1,0:T(8,128)(2,1)} %get-tuple-element.10.refs_2_, ...), custom_call_target="tpu_custom_call" | custom-call | tf_op jit(solution)/shard_map/pallas_call | solution.py:551

commit v3 on v2

--- a/solution.py
+++ b/solution.py
@@ -19,7 +19,7 @@
 DIRS = (1, -1)
 FAR_FIRST = (4, 3, 5, 2, 6, 1, 7, 0)
 VMEM_BYTES = 62 << 20
-SEND_SEMS, RECV_SEMS = 7, 84
+SEND_SEMS, RECV_SEMS = 7, 112
 
 
 def sigmoid_parts(gate, up):
@@ -72,7 +72,7 @@
 def kernel(
     gate_hbm, up_hbm, cot_hbm, w_hbm, slot_ref, live_ref,
     proj_hbm, gate_out_hbm, up_out_hbm, tile_hbm,
-    proj_ref, gate_out, up_out, tile_out, gate_ref, up_ref, wbuf, cbuf, sbuf, sscal, invv, inv, hid, hid_t, terms, tsib, zrecv, xrecv, pbuf, yrecv, lrecv,
+    proj_ref, gate_out, up_out, tile_out, gate_ref, up_ref, wbuf, cbuf, sbuf, sscal, invv, inv, hid, hid_t, terms, tsib, zrecv, xrecv, pbuf, yrecv, lrecv, zfirst, yfirst,
     ssem, rsem, lsem,
 ):
     d, t = lax.axis_index("dp"), lax.axis_index("tensor")
@@ -115,11 +115,13 @@
         which = xh if part == 0 else 1 - xh
         return wbuf.at[pl.ds((((pos * 2) + which) * 2 + c) * OWN + first, count)]
 
-    def last_hop(way, part):
-        return 3 if part == (0 if way == 1 else 1) else 2
-
-    def ways_of(k, part):
-        return [way for way in DIRS if k <= last_hop(way, part)]
+    def gather_ways(count, k, part, i):
+        if part == 1:
+            return DIRS if k < 3 else ()
+        return DIRS if k < 3 else (half_way(count, i),) if k == 3 else ()
+
+    def half_way(count, i):
+        return 1 if i < (count + 1) // 2 else -1
 
     def tile_send(way, k, part, i):
         ref = tiles(at(z, -way * k), part, i, 1)
@@ -129,14 +131,26 @@
         ref = tiles(pos, part)
         traffic.send("K", 0, ref, ref, on_core)
 
+    def tile_cores(k, part):
+        for way in DIRS if k < 3 else (1,):
+            tile_core(at(z, -way * (k + 1)), part)
+
     def tile_event(k, part, i):
-        ways = ways_of(k, part)
+        ways = gather_ways(OWN, k, part, i)
         traffic.arrive("A", (k, part, i), wbuf.at[pl.ds(0, len(ways))])
-        for way in ways_of(k + 1, part):
+        for way in gather_ways(OWN, k + 1, part, i):
             tile_send(way, k + 1, part, i)
+        if part == 0 and k == 3:
+            for way in ways:
+                ref = tiles(at(z, -way * (k + 1)), 0, i, 1)
+                traffic.send("A", ("far", i), ref, ref, on_x_hi)
         if i == OWN - 1:
-            for way in ways:
-                tile_core(at(z, -way * (k + 1)), part)
+            tile_cores(k, part)
+
+    def tile_far_event(i):
+        traffic.arrive("A", ("far", i), wbuf.at[pl.ds(0, 1)])
+        if i == OWN - 1:
+            tile_cores(3, 1)
 
     def tile_x_event(i):
         traffic.arrive("A", ("x", i), wbuf.at[pl.ds(0, 1)])
@@ -154,9 +168,17 @@
         traffic.send("C", (k, part, i), ref, ref, on_y(way))
 
     def col_event(k, part, i):
-        traffic.arrive("C", (k, part, i), cbuf.at[pl.ds(0, len(ways_of(k, part)))])
-        for way in ways_of(k + 1, part):
+        ways = gather_ways(2, k, part, i)
+        traffic.arrive("C", (k, part, i), cbuf.at[pl.ds(0, len(ways))])
+        for way in gather_ways(2, k + 1, part, i):
             col_send(way, k + 1, part, i)
+        if part == 0 and k == 3:
+            for way in ways:
+                ref = column(at(y, -way * (k + 1)), 0, i)
+                traffic.send("C", ("far", i), ref, ref, on_x_lo)
+
+    def col_far_event(i):
+        traffic.arrive("C", ("far", i), cbuf.at[pl.ds(0, 1)])
 
     def col_x_event(i):
         traffic.arrive("C", ("x", i), cbuf.at[pl.ds(0, 1)])
@@ -213,38 +235,36 @@
 
     tile_event(0, 0, 0)
     col_event(0, 0, 0)
+    row_z_event()
     col_x_event(0)
     tile_event(0, 0, 1)
+    tile_x_event(0)
     col_event(0, 0, 1)
     col_x_event(1)
-    tile_x_event(0)
     tile_event(0, 0, 2)
-    row_z_event()
     tile_x_event(1)
     tile_x_event(2)
     tile_event(1, 0, 0)
     col_event(1, 0, 0)
+    row_x_event()
+    tile_event(1, 0, 1)
     col_event(0, 1, 0)
-    tile_event(1, 0, 1)
+    tile_event(0, 1, 0)
     col_event(1, 0, 1)
-    tile_event(0, 1, 0)
-    row_x_event()
-    col_event(0, 1, 1)
-    tile_event(1, 0, 2)
-    tile_event(0, 1, 1)
-    col_event(2, 0, 0)
-    tile_event(0, 1, 2)
-    col_event(1, 1, 0)
     traffic.arrive("S", "core", rows(0, 2 * RING))
     to_scalar = pltpu.make_async_copy(sbuf, sscal, lsem.at[0])
     to_scalar.start()
+    tile_event(1, 0, 2)
+    col_event(0, 1, 1)
+    tile_event(0, 1, 1)
+    tile_event(0, 1, 2)
+    col_event(2, 0, 0)
+    col_event(1, 1, 0)
+    tile_event(2, 0, 0)
     col_event(2, 0, 1)
-    tile_event(2, 0, 0)
+    tile_event(2, 0, 1)
+    tile_event(1, 1, 0)
     col_event(1, 1, 1)
-    tile_event(2, 0, 1)
-    col_event(3, 0, 0)
-    tile_event(1, 1, 0)
-    col_event(2, 1, 0)
     tile_event(2, 0, 2)
     to_scalar.wait()
 
@@ -265,26 +285,34 @@
     to_inv = pltpu.make_async_copy(invv, inv, lsem.at[1])
     to_inv.start()
 
+    col_event(3, 0, 0)
+    tile_event(1, 1, 1)
+    col_event(2, 1, 0)
+    tile_event(1, 1, 2)
     col_event(3, 0, 1)
-    tile_event(1, 1, 1)
+    tile_event(3, 0, 0)
     col_event(2, 1, 1)
-    tile_event(1, 1, 2)
-    tile_event(3, 0, 0)
-    col_event(3, 1, 0)
-    col_event(3, 1, 1)
+    tile_event(3, 0, 1)
+    tile_event(3, 0, 2)
+    col_far_event(0)
+    tile_event(2, 1, 0)
+    tile_event(2, 1, 1)
+    col_far_event(1)
 
     def group(owner_z, core, add):
         for owner_x in range(2):
             row = row_of(owner_z, owner_x, core)
+            first = ((owner_z * 2 + owner_x) * 2 + core) * OWN
+            index = (owner_z * 2 + owner_x) * OWN
+            slots = [sscal[row, 0, j] for j in range(OWN)]
+            left = [hid_t[slot // MODEL] for slot in slots]
+            right = [cbuf[lax.rem(slot, MODEL)] for slot in slots]
+            dots = [jnp.dot(a, b, preferred_element_type=F32) for a, b in zip(left, right)]
             for j in range(OWN):
-                slot = sscal[row, 0, j]
-                s = ((owner_z * 2 + owner_x) * 2 + core) * OWN + j
-                factor = jnp.where(s < live, SCALE, 0.0)
-                term = jnp.dot(hid_t[slot // MODEL], cbuf[lax.rem(slot, MODEL)], preferred_element_type=F32) * factor
-                index = (owner_z * 2 + owner_x) * OWN + j
+                term = dots[j] * jnp.where(first + j < live, SCALE, 0.0)
                 if add:
-                    term += tsib[index].astype(F32)
-                terms[core * 48 + index] = term.astype(BF)
+                    term += tsib[index + j].astype(F32)
+                terms[core * 48 + index + j] = term.astype(BF)
 
     def for_sibling(n):
         owner_z = at(z, FAR_FIRST[n])
@@ -297,89 +325,94 @@
         traffic.arrive("T", n, tsib.at[pl.ds(0, 6)])
         group(at(z, FAR_FIRST[n]), c, True)
 
-    def z_local(pos, part):
+    class Scatter:
+        def __init__(self, family, count, local, recv, first, index, pos, on_ring, on_x):
+            self.family, self.count, self.local, self.recv, self.first = family, count, local, recv, first
+            self.index, self.pos, self.on_ring, self.on_x = index, pos, on_ring, on_x
+
+        def mine(self, step, part, i):
+            return self.local.at[self.index(at(self.pos, step), part, i)]
+
+        def like(self, n):
+            return self.local.at[pl.ds(0, n)]
+
+        def to_x(self, n):
+            for i in range(self.count):
+                traffic.send(
+                    self.family, ("first", n, i), self.mine((4, 3, -3)[n], 0, i), self.first.at[n, pl.ds(i, 1)], self.on_x
+                )
+
+        def from_x(self, n):
+            for i in range(self.count):
+                traffic.arrive(self.family, ("first", n, i), self.like(1))
+                mine = self.mine((4, 3, -3)[n], 1, i)
+                mine[...] = (mine[...].astype(F32) + self.first[n, pl.ds(i, 1)].astype(F32)).astype(BF)
+
+        def place(self, way, k, part, i):
+            return self.recv.at[0 if way == 1 else 1, k, part, pl.ds(i, 1)]
+
+        def send(self, way, k, part, i, src):
+            traffic.send(self.family, (k, part, i), src, self.place(way, k, part, i), self.on_ring(way))
+
+        def fresh(self, k, part):
+            for i in range(self.count):
+                far = half_way(self.count, i)
+                for way in {0: (far,), 1: (-far,), 2: DIRS}[k]:
+                    self.send(way, k, part, i, self.mine(way * (4 - k), part, i))
+
+        def event(self, k, part, i):
+            ways = (half_way(self.count, i),) if k == 0 else DIRS
+            traffic.arrive(self.family, (k, part, i), self.like(len(ways)))
+            if k < 3:
+                for way in ways:
+                    held = self.place(way, k, part, i)
+                    held[...] = (held[...].astype(F32) + self.mine(way * (3 - k), part, i)[...].astype(F32)).astype(BF)
+                    self.send(way, k + 1, part, i, held)
+
+        def total(self, part, i):
+            return (
+                self.place(1, 3, part, i)[...].astype(F32)
+                + self.place(-1, 3, part, i)[...].astype(F32)
+                + self.mine(0, part, i)[...].astype(F32)
+            )
+
+        def hand_over(self, i, dst):
+            mine = self.mine(0, 0, i)
+            mine[...] = self.total(0, i).astype(BF)
+            traffic.send(self.family, ("x", i), mine, dst.at[pl.ds(i, 1)], self.on_x)
+
+        def whole(self, i, dst):
+            traffic.arrive(self.family, ("x", i), self.like(1))
+            return (self.total(1, i) + dst[pl.ds(i, 1)].astype(F32))[0]
+
+    def z_local(pos, part, i):
         which = 1 - xh if part == 0 else xh
-        return pl.ds(c * 48 + (pos * 2 + which) * OWN, OWN)
+        return pl.ds(c * 48 + (pos * 2 + which) * OWN + i, 1)
 
     def y_local(pos, part, i):
         which = 1 - xl if part == 0 else xl
         return pl.ds((which * RING + pos) * 2 + i, 1)
 
-    def y_fresh(way, k, part):
-        side = 0 if way == 1 else 1
-        for i in range(2):
-            src = pbuf.at[y_local(at(y, way * (4 - k)), part, i)]
-            traffic.send("B", (k, part if way == 1 else 1 - part, i), src, yrecv.at[side, k, part, pl.ds(i, 1)], on_y(way))
-
-    def z_key(way, k, part):
-        return (k, part if way == 1 else 1 - part)
-
-    def z_start():
-        for k in range(2):
-            for way in DIRS:
-                part = k if way == 1 else 1 - k
-                src = terms.at[z_local(at(z, way * (4 - k)), part)]
-                side = 0 if way == 1 else 1
-                traffic.send("D", z_key(way, k, part), src, zrecv.at[side, k, part], on_z(way))
-
-    def z_event(n):
-        k, lead = (n + 1) // 2, n % 2
-        traffic.arrive("D", (k, lead), terms.at[pl.ds(0, 2 * OWN)])
-        for way in DIRS:
-            part = lead if way == 1 else 1 - lead
-            side = 0 if way == 1 else 1
-            if k < 3:
-                here = z_local(at(z, way * (3 - k)), part)
-                zrecv[side, k, part] = (zrecv[side, k, part].astype(F32) + terms[here].astype(F32)).astype(BF)
-                traffic.send(
-                    "D", z_key(way, k + 1, part), zrecv.at[side, k, part], zrecv.at[side, k + 1, part], on_z(way)
-                )
-
-    def z_total(part):
-        return (
-            zrecv[0, 3, part].astype(F32) + zrecv[1, 3, part].astype(F32) + terms[z_local(z, part)].astype(F32)
-        )
-
-    def y_start(k):
-        for way in DIRS:
-            y_fresh(way, k, k if way == 1 else 1 - k)
-
-    def y_event(n, i):
-        k, lead = (n + 1) // 2, n % 2
-        traffic.arrive("B", (k, lead, i), pbuf.at[pl.ds(0, 2)])
-        for way in DIRS:
-            part = lead if way == 1 else 1 - lead
-            side = 0 if way == 1 else 1
-            if k < 3:
-                here = y_local(at(y, way * (3 - k)), part, i)
-                held = yrecv.at[side, k, part, pl.ds(i, 1)]
-                held[...] = (held[...].astype(F32) + pbuf[here].astype(F32)).astype(BF)
-                traffic.send("B", (k + 1, lead, i), held, yrecv.at[side, k + 1, part, pl.ds(i, 1)], on_y(way))
-
-    def y_total(part, i):
-        return (
-            yrecv[0, 3, part, i].astype(F32) + yrecv[1, 3, part, i].astype(F32)
-            + pbuf[y_local(y, part, i)][0].astype(F32)
-        )
-
-    for_sibling(0)
-    for_sibling(1)
-    for_sibling(2)
-    tile_event(3, 0, 1)
-    tile_event(2, 1, 0)
-    for_own(0)
-    for_own(1)
-    for_own(2)
-    tile_event(3, 0, 2)
-    tile_event(2, 1, 1)
+    grads = Scatter("D", OWN, terms, zrecv, zfirst, z_local, z, on_z, on_x_hi)
+    sums = Scatter("B", 2, pbuf, yrecv, yfirst, y_local, y, on_y, on_x_lo)
+
+    for n in range(3):
+        for_sibling(n)
     tile_event(2, 1, 2)
-    z_start()
-    for n in range(3, 8):
+    for n in range(3):
+        for_own(n)
+        grads.to_x(n)
+    tile_far_event(0)
+    for_sibling(3)
+    for_sibling(4)
+    tile_far_event(1)
+    tile_far_event(2)
+    for_own(3)
+    for_own(4)
+    grads.fresh(2, 0)
+    for n in range(5, 8):
         for_sibling(n)
-    tile_event(3, 1, 0)
-    tile_event(3, 1, 1)
-    tile_event(3, 1, 2)
-    for n in range(3, 6):
+    for n in range(5, 8):
         for_own(n)
     to_inv.wait()
     traffic.arrive("K", 0, wbuf.at[pl.ds(0, 48)])
@@ -416,60 +449,64 @@
         gate_out[:, piece] = (grad * up_val * sig * (1.0 + gate_val * (1.0 - sig))).astype(BF)
         up_out[:, piece] = (grad * (gate_val * sig)).astype(BF)
 
-    forward_of(4, 0)
+    for n in range(3):
+        forward_of((4, 3, -3)[n], 0)
+        sums.to_x(n)
+    for n in range(3):
+        grads.from_x(n)
+        if n == 0:
+            grads.fresh(0, 1)
+    grads.fresh(1, 1)
+    forward_of(2, 0)
+    forward_of(-2, 0)
+    sums.fresh(2, 0)
+    for i in range(OWN):
+        grads.event(2, 0, i)
     forward_of(4, 1)
-    y_start(0)
     forward_of(3, 1)
-    forward_of(-3, 0)
-    y_start(1)
-    z_event(0)
-    for_own(6)
-    for_own(7)
-    forward_of(3, 0)
     forward_of(-3, 1)
-
-    def rest(i, _):
-        step = (2 - i // 2) * (1 - 2 * lax.rem(i, 2))
-        forward_of(step, 0)
-        forward_of(step, 1)
-        return 0
-
-    lax.fori_loop(0, 4, rest, 0)
-    z_event(1)
-    y_event(0, 0)
-    y_event(0, 1)
-    y_event(1, 0)
-    y_event(1, 1)
+    for n in range(3):
+        sums.from_x(n)
+        if n == 0:
+            sums.fresh(0, 1)
+    sums.fresh(1, 1)
+    for i in range(OWN):
+        grads.event(0, 1, i)
+    forward_of(1, 0)
+    forward_of(-1, 0)
+    for i in range(2):
+        sums.event(2, 0, i)
+    forward_of(2, 1)
+    forward_of(-2, 1)
+    for i in range(OWN):
+        grads.event(3, 0, i)
+        grads.hand_over(i, xrecv)
+    for i in range(2):
+        sums.event(0, 1, i)
     forward_of(0, 0)
+    forward_of(1, 1)
+    backward(2, 2)
+    for i in range(OWN):
+        grads.event(1, 1, i)
+    for i in range(2):
+        sums.event(3, 0, i)
+        sums.hand_over(i, lrecv)
+    forward_of(-1, 1)
+    for i in range(2):
+        sums.event(1, 1, i)
     forward_of(0, 1)
-    z_event(2)
-    y_event(2, 0)
-    y_event(2, 1)
-    y_event(3, 0)
-    z_event(3)
-    y_event(3, 1)
-    y_event(4, 0)
-    y_event(4, 1)
-    z_event(4)
-    y_event(5, 0)
-    y_event(5, 1)
     backward(0, 2)
-    z_event(5)
+    for i in range(OWN):
+        grads.event(2, 1, i)
     for i in range(2):
-        y_event(6, i)
-        there = y_local(y, 0, i)
-        pbuf[there] = y_total(0, i).astype(BF)[None]
-        traffic.send("B", ("x", i), pbuf.at[there], lrecv.at[pl.ds(i, 1)], on_x_lo)
-    backward(2, 2)
-    z_event(6)
-    there = z_local(z, 0)
-    terms[there] = z_total(0).astype(BF)
-    traffic.send("D", "x", terms.at[there], xrecv, on_x_hi)
+        sums.event(2, 1, i)
     backward(4, 2)
     backward(6, 1)
+    for i in range(OWN):
+        grads.event(3, 1, i)
     for i in range(2):
-        traffic.arrive("B", ("x", i), lrecv.at[pl.ds(0, 1)])
-        proj_ref[:, i * EDGE : (i + 1) * EDGE] = (y_total(1, i) + lrecv[i].astype(F32)).astype(BF)
+        sums.event(3, 1, i)
+        proj_ref[:, i * EDGE : (i + 1) * EDGE] = sums.whole(i, lrecv).astype(BF)
     stores = [
         pltpu.make_async_copy(gate_out, gate_out_hbm, lsem.at[0]),
         pltpu.make_async_copy(up_out, up_out_hbm, lsem.at[1]),
@@ -484,8 +521,8 @@
     traffic.left("C", cbuf.at[pl.ds(0, 30)])
     traffic.left("T", tsib.at[pl.ds(0, 48)])
     traffic.left("B", pbuf.at[pl.ds(0, 30)])
-    traffic.arrive("D", "x", xrecv)
-    tile_out[0] = z_total(1) + xrecv[...].astype(F32)
+    for i in range(OWN):
+        tile_out[0, i] = grads.whole(i, xrecv)
     stores[3].start()
     traffic.left("D", terms.at[pl.ds(0, 45)])
     for store in stores:
@@ -540,6 +577,8 @@
             pltpu.VMEM((MODEL, *tile), BF),
             pltpu.VMEM((2, 4, 2, 2, *tile), BF),
             pltpu.VMEM((2, *tile), BF),
+            pltpu.VMEM((3, OWN, *tile), BF),
+            pltpu.VMEM((3, 2, *tile), BF),
             pltpu.SemaphoreType.DMA((SEND_SEMS,)),
             pltpu.SemaphoreType.DMA((RECV_SEMS,)),
             pltpu.SemaphoreType.DMA((5,)),

time: 67.3 us -> 66.3 us (0.985)
  Pallas kernels: 65.8 us -> 64.6 us
    pallas_call x1, Pallas kernels: 63.9 us -> 62.7 us  [per_device(): pl.pallas_call(kernel, out_shape=shapes, in_specs=[hbm] * 4 + [smem] * 2,...]
where the time goes in v3:
time: 66.3 us; the launch traced here: 65.9 us
  Pallas kernels  64.6 us (97%)
  between operations  1.29 us (2%)
    pallas_call x1, Pallas kernels, per_device(): pl.pallas_call(kernel, out_shape=shapes, in_specs=[hbm] * 4 + [smem] * 2,...  62.7 us
    pallas_call x1, Pallas kernels, per_device(): pl.pallas_call(hand_out, out_shape=shapes, in_specs=[hbm] * 4, out_specs=...  1.93 us

profile of v3, /device:TPU:1, one launch (start us, length us, event | category | flops | bytes accessed | tf_op | source)
XLA Modules:
  0.0 65.9 jit_solution(8324887382045295128)
XLA Ops:
  1.3 62.7 %shard_map.93 = (bf16[128,256]{1,0:T(8,128)(2,1)}, bf16[128,896]{1,0:T(8,128)(2,1)}, bf16[128,896]{1,0:T(8,128)(2,1)}, f32[1,3,128,128]{3,2,1,0:T(8,128)}) custom-call(bf16[128,896]{1,0:T(8,128)(2,1)} %gate_hbm.1, bf16[128,896]{1,0:T(8,128)(2,1)} %up_hbm.1, bf16[128,256]{1,0:T(8,128)(2,1)} %cot_hbm.1, bf16[1,3,128,128]{3,2,1,0:T(8,128)(2,1)} %w_hbm.1, ...), custom_call_target="tpu_custom_call" | custom-call | tf_op jit(solution)/shard_map/pallas_call | solution.py:556
  64.0 1.9 %shard_map.94 = (bf16[128,256]{1,0:T(8,128)(2,1)}, bf16[128,896]{1,0:T(8,128)(2,1)}, bf16[128,896]{1,0:T(8,128)(2,1)}, f32[1,3,128,128]{3,2,1,0:T(8,128)}) custom-call(bf16[128,256]{1,0:T(8,128)(2,1)} %get-tuple-element.8.refs_0_, bf16[128,896]{1,0:T(8,128)(2,1)} %get-tuple-element.9.refs_1_, bf16[128,896]{1,0:T(8,128)(2,1)} %get-tuple-element.10.refs_2_, ...), custom_call_target="tpu_custom_call" | custom-call | tf_op jit(solution)/shard_map/pallas_call | solution.py:590
